TPU v7x, 32 devices: a whole 2x2x4 slice. The times are simulated.
32 devices in a mesh: groups: 2 (over x), blk: 16 (over z, y, core).
Axes of the slice: x: 2, y: 2, z: 4, core: 2. Of those that a mesh axis runs over, the one named last changes fastest.
Arguments:
- walkers: bfloat16 [192, 256, 128], P(('groups', 'blk')), parts along dimension 0, may hold values from -6 to 6
- inv_intersection: bfloat16 [192, 128, 128], P(('groups', 'blk')), parts along dimension 0, may hold values from -0.5 to 0.5
- trial_orbs: bfloat16 [256, 128], replicated, may hold values from -0.375 to 0.375
- cholesky: bfloat16 [4096, 256, 256], P(('groups', 'blk')), parts along dimension 0, may hold values from -0.02734375 to 0.02734375
- aux_fields: float32 [192, 2048], P('groups', 'blk'), parts along dimension 0, may hold values from -6 to 6
Outputs:
- new_walkers: bfloat16 [192, 256, 128], P(('groups', 'blk')), parts along dimension 0
- intersection: float32 [192, 128, 128], P(('groups', 'blk')), parts along dimension 0
There are 2 independent parts, one for each index of `groups`. A program takes and returns all parts, laid end to end along the dimension named above; an argument that names none is the same for every part. Nothing has to cross between parts.
All inputs are finite; a program needn't handle non-finite values.
Results may differ from a plain program's by a relative error of at most 0.018.
Values may be sent and summed in bfloat16 or wider, within the bound.
A program may use at most 192 MiB of HBM per device.

v0:
```python
import jax
import jax.numpy as jnp
from jax import lax
from jax.sharding import PartitionSpec as P

root_step = 0.1
bias_step = 0.5


def body(walkers, inv_intersection, trial_orbs, cholesky, aux_fields):
    f32 = jnp.float32
    rotated = jnp.einsum(
        "wpi,wij->wpj", walkers, inv_intersection, preferred_element_type=f32
    ).astype(jnp.bfloat16)
    own_half = jnp.einsum("pi,gpq->giq", trial_orbs, cholesky, preferred_element_type=f32).astype(
        jnp.bfloat16
    )
    everyone = lax.all_gather(rotated, "blk", axis=0, tiled=True)
    force_bias = jnp.einsum("giq,wqi->wg", own_half, everyone, preferred_element_type=f32)
    shifted = (aux_fields + bias_step * force_bias).astype(jnp.bfloat16)
    terms = jnp.einsum("wg,gpq->wpq", shifted, cholesky, preferred_element_type=f32)
    summed_pot = lax.psum_scatter(
        terms.astype(jnp.bfloat16), "blk", scatter_dimension=0, tiled=True
    ).astype(jnp.float32)
    potential = (root_step * summed_pot).astype(jnp.bfloat16)
    taylor_term = walkers
    summed = walkers.astype(f32)
    for degree in range(1, 5):
        product = jnp.einsum("wpq,wqi->wpi", potential, taylor_term, preferred_element_type=f32)
        taylor_term = (product / degree).astype(jnp.bfloat16)
        summed = summed + taylor_term.astype(f32)
    new_walkers = summed.astype(jnp.bfloat16)
    intersection = jnp.einsum("pi,wpj->wij", trial_orbs, new_walkers, preferred_element_type=f32)
    return (new_walkers, intersection)


def solution(mesh):
    return jax.shard_map(
        body,
        mesh=mesh,
        in_specs=(
            P(("groups", "blk"), None, None),
            P(("groups", "blk"), None, None),
            P(),
            P(("groups", "blk"), None, None),
            P("groups", "blk"),
        ),
        out_specs=(P(("groups", "blk"), None, None), P(("groups", "blk"), None, None)),
        check_vma=False,
    )
```

profile of v0, /device:TPU:0, one launch (start us, length us, event | category | flops | bytes accessed | tf_op | source)
XLA Modules:
  0.0 273.0 jit_solution(14691746136520215)
XLA Ops:
  7.2 0.0 copy-start
  7.2 0.0 all-gather.2.cloned.1.call-start
  7.2 0.9 copy-done
  8.1 2.0 convolution_convert_fusion.1
  10.1 0.0 all-gather.2.cloned.1.call-update
  10.1 0.0 reduce-scatter.2.cloned.1.call-start
  10.2 13.6 %convert_bitcast_fusion = bf16[128,128,256]{1,2,0:T(8,128)(2,1)} fusion(bf16[128,256,256]{2,1,0:T(8,128)(2,1)} %param.8, bf16[256,128]{1,0:T(8,128)(2,1)} %param.7), kind=kOutput, calls=%fused_computation.2 | convolution fusion | flops 2151677952 | bytes 25231360 | tf_op jit(solution)/shard_map/pi,gpq->giq/dot_general | solution.py:15
  23.8 13.0 %copy.19 = bf16[128,128,256]{0,2,1:T(8,128)(2,1)} copy(bf16[128,128,256]{1,2,0:T(8,128)(2,1)} %convert_bitcast_fusion) | data formatting | bytes 16777216 | tf_op jit(solution)/shard_map/convert_element_type | solution.py:15
  36.8 38.7 %all-gather.2.cloned.1.call-done = bf16[96,256,128]{2,1,0:T(8,128)(2,1)} async-done(((bf16[6,256,128]{2,1,0:T(8,128)(2,1)}), bf16[96,256,128]{2,1,0:T(8,128)(2,1)}) %all-gather.2.cloned.1.call-update) | async-done | bytes 6291472 | tf_op jit(solution)/shard_map/all_gather | solution.py:18
  75.5 9.0 %copy.18 = bf16[96,256,128]{1,0,2:T(8,128)(2,1)} copy(bf16[96,256,128]{2,1,0:T(8,128)(2,1)} %all-gather.2.cloned.1.call-done) | data formatting | bytes 12582912 | tf_op jit(solution)/shard_map/all_gather | solution.py:18
  84.5 0.0 copy-done.5
  84.5 7.2 %fusion.14 = bf16[96,128,1]{1,0,2:T(8,128)(2,1)S(1)} fusion(f32[96,128]{1,0:T(8,128)S(1)} %copy-done.5, bf16[96,256,128]{1,0,2:T(8,128)(2,1)} %copy.18, bf16[128,128,256]{0,2,1:T(8,128)(2,1)} %copy.19), kind=kOutput, calls=%fused_computation.21 | convolution fusion | flops 805343232 | bytes 14753792 | tf_op jit(solution)/shard_map/giq,wqi->wg/dot_general | solution.py:19
  91.7 21.0 %fusion.2 = bf16[96,256,256]{2,0,1:T(8,128)(2,1)} fusion(bf16[96,128,1]{1,0,2:T(8,128)(2,1)S(1)} %fusion.14, bf16[128,256,256]{2,1,0:T(8,128)(2,1)} %param.8), kind=kOutput, calls=%fused_computation.3 | convolution fusion | flops 1616904192 | bytes 29384704 | tf_op jit(solution)/shard_map/wg,gpq->wpq/dot_general | solution.py:21
  112.7 12.5 %copy.15 = bf16[96,256,256]{2,1,0:T(8,128)(2,1)} copy(bf16[96,256,256]{2,0,1:T(8,128)(2,1)} %fusion.2) | data formatting | bytes 25165824 | tf_op jit(solution)/shard_map/convert_element_type | solution.py:23
  125.2 0.0 reduce-scatter.2.cloned.1.call-update
  125.3 133.5 %reduce-scatter.2.cloned.1.call-done = bf16[6,256,256]{2,1,0:T(8,128)(2,1)} async-done(((bf16[96,256,256]{2,1,0:T(8,128)(2,1)}), bf16[6,256,256]{2,1,0:T(8,128)(2,1)}) %reduce-scatter.2.cloned.1.call-update) | async-done | bytes 786448 | tf_op jit(solution)/shard_map/reduce_scatter | solution.py:22
  258.8 1.5 convolution_convert_fusion
  260.3 1.5 fusion.5
  261.8 1.5 fusion.6
  263.3 1.6 fusion.10
  264.9 0.0 copy-start.3
  264.9 0.3 convolution_bitcast_fusion
  265.2 0.9 copy.17
  266.2 0.0 copy-done.1
  (7 shorter events, 0.0 us)
Async XLA Ops:
  7.2 0.9 copy-start
  7.2 68.3 %all-gather.2.cloned.1.call-start = ((), (), s32[]{:S(2)}) async-start(), calls=%async_computation.1 | async-start | bytes 6684672 | tf_op jit(solution)/shard_map/all_gather | solution.py:18
  10.1 248.7 %reduce-scatter.2.cloned.1.call-start = ((), (), s32[]{:S(2)}) async-start(), calls=%async_computation.2 | async-start | bytes 13369344 | tf_op jit(solution)/shard_map/reduce_scatter | solution.py:22
  36.7 47.7 %copy-start.5 = (f32[96,128]{1,0:T(8,128)S(1)}, f32[96,128]{1,0:T(8,128)}, u32[]{:S(2)}) copy-start(f32[96,128]{1,0:T(8,128)} %param.9) | copy-start | bytes 147460
  125.2 133.6 %copy-start.2 = (bf16[6,256,128]{2,1,0:T(8,128)(2,1)S(1)}, bf16[6,256,128]{2,1,0:T(8,128)(2,1)}, u32[]{:S(2)}) copy-start(bf16[6,256,128]{2,1,0:T(8,128)(2,1)} %param.5) | copy-start | bytes 1179652
  125.2 140.9 %copy-start.1 = (bf16[6,128,128]{2,1,0:T(8,128)(2,1)S(1)}, bf16[6,128,128]{2,1,0:T(8,128)(2,1)}, u32[]{:S(2)}) copy-start(bf16[6,128,128]{2,1,0:T(8,128)(2,1)} %param.6) | copy-start | bytes 589828
  125.2 139.7 %copy-start.4 = (bf16[256,128]{1,0:T(8,128)(2,1)S(1)}, bf16[256,128]{1,0:T(8,128)(2,1)}, u32[]{:S(2)}) copy-start(bf16[256,128]{1,0:T(8,128)(2,1)} %param.7) | copy-start | bytes 196612
  264.9 1.2 copy-start.3
Sparse Core Ops, SparseCore 0:
  10.9 64.5 all-gather.1
  125.4 133.3 reduce-scatter.1
where the time goes:
time: 274 us; the launch traced here: 273 us
  waiting for transfers between devices  172 us (63%)
  matrix products  50.2 us (18%)
  local copies, waits for them, and re-layouts  36.3 us (13%)
  between operations  14.1 us (5%)
    reduce_scatter x1, waiting for transfers between devices, body(): lax.psum_scatter(terms.astype(jnp.bfloat16), 'blk', scatter_dimension=0,...  134 us
    all_gather x1, waiting for transfers between devices, body(): everyone = lax.all_gather(rotated, 'blk', axis=0, tiled=True)  38.7 us
    dot_general x1, matrix products, body(): jnp.einsum('wg,gpq->wpq', shifted, cholesky, preferred_element_type=f32)  21 us
    dot_general x1, matrix products, body(): jnp.einsum('pi,gpq->giq', trial_orbs, cholesky, preferred_element_type=f32)  13.6 us
    convert_element_type x1, local copies, waits for them, and re-layouts, body(): jnp.einsum('pi,gpq->giq', trial_orbs, cholesky, preferred_element_type=f32)  13 us
    convert_element_type x1, local copies, waits for them, and re-layouts, body(): terms.astype(jnp.bfloat16)  12.5 us
    all_gather x1, local copies, waits for them, and re-layouts, body(): everyone = lax.all_gather(rotated, 'blk', axis=0, tiled=True)  9.02 us
    dot_general x1, matrix products, body(): jnp.einsum('giq,wqi->wg', own_half, everyone, preferred_element_type=f32)  7.23 us
  transfers between devices with their start and end apart: 2, of which 2 were waited for; matrix products, arithmetic and copies ran while one was open for 10% of the time, Pallas kernels for 0%

commit v1 on v0

v1 whole, which is shorter than its diff:
```python
import functools

import jax
import jax.numpy as jnp
import numpy as np
from jax import lax
from jax.experimental import pallas as pl
from jax.experimental.pallas import tpu as pltpu
from jax.sharding import PartitionSpec as P

root_step = 0.1
bias_step = 0.5
MESH = pl.DeviceIdType.MESH
bf16 = jnp.bfloat16
f32 = jnp.float32


def row_orders(planes):
    half = planes * 12
    order = np.zeros((2, 2, half), np.int64)
    for parity in range(2):
        for y in range(2):
            for m in range(half):
                if m < planes * 8:
                    dest, within = m // 8, m % 8
                else:
                    rest = m - planes * 8
                    side = (rest % 8) // 4
                    dest = 2 * (rest // 8) + (side if parity == 0 else 1 - side)
                    within = 8 + rest % 4
                order[parity, y, m] = (dest * 2 + y) * 12 + within
    return order.reshape(-1)[:, None] == np.arange(2 * half)[None, :]


def scatter_kernel(planes, chunks, s_ref, perm_ref, chol_ref, out_ref,
                   sib_s, sp, chol2, ysend, held, up, down,
                   s_sem, load_sem, chol_send, chol_recv, y_send, y_recv,
                   up_send, up_recv, down_send, down_recv, out_send, out_recv):
    norb, own_g, _ = chol_ref.shape
    span = norb // chunks
    rows = span * 12
    half = planes * 12
    me = lax.axis_index("blk")
    core = lax.rem(me, 2)
    y = lax.rem(lax.div(me, 2), 2)
    z = lax.div(me, 4)
    sibling = me + 1 - 2 * core
    across = me + 2 - 4 * y
    above = me + 4
    below = me - 4
    not_first, not_last = z > 0, z < planes - 1

    barrier = pltpu.get_barrier_semaphore()
    pl.semaphore_signal(barrier, inc=1, device_id={"blk": sibling}, device_id_type=MESH)
    pl.semaphore_signal(barrier, inc=1, device_id={"blk": across}, device_id_type=MESH)

    @pl.when(not_first)
    def _():
        pl.semaphore_signal(barrier, inc=1, device_id={"blk": below}, device_id_type=MESH)

    @pl.when(not_last)
    def _():
        pl.semaphore_signal(barrier, inc=1, device_id={"blk": above}, device_id_type=MESH)

    peers = 2 + jnp.where(not_first, 1, 0) + jnp.where(not_last, 1, 0)
    pl.semaphore_wait(barrier, peers)

    def remote(src, dst, send, recv, target):
        return pltpu.make_async_remote_copy(
            src_ref=src, dst_ref=dst, send_sem=send, recv_sem=recv,
            device_id={"blk": target}, device_id_type=MESH)

    def chol_load(k):
        return pltpu.make_async_copy(
            chol_ref.at[pl.ds(k * span, span), :, pl.ds(pl.multiple_of(core * 128, 128), 128)],
            chol2.at[pl.ds(k * span, span), pl.ds(0, own_g)], load_sem.at[k])

    def chol_swap(k):
        return remote(
            chol_ref.at[pl.ds(k * span, span), :, pl.ds(pl.multiple_of((1 - core) * 128, 128), 128)],
            chol2.at[pl.ds(k * span, span), pl.ds(own_g, own_g)],
            chol_send.at[k], chol_recv.at[k], sibling)

    def y_copy(k):
        return remote(ysend.at[k], held.at[k], y_send.at[k], y_recv.at[k], across)

    def out_copy(k):
        piece = out_ref.at[core, pl.ds(pl.multiple_of(k * rows, 16), rows)]
        return remote(piece, piece, out_send.at[k], out_recv.at[k], sibling)

    s_copy = remote(s_ref, sib_s, s_sem.at[0], s_sem.at[1], sibling)
    s_copy.start()

    def begin(k, carry):
        chol_load(k).start()
        chol_swap(k).start()
        return carry

    lax.fori_loop(0, chunks, begin, 0)
    s_copy.wait()
    for parity in range(2):
        for side in range(2):
            pick = perm_ref[pl.ds((parity * 2 + side) * half, half), :]
            sp[parity, side, :, 0:own_g] = jnp.dot(
                pick, s_ref[...], preferred_element_type=f32).astype(bf16)
            sp[parity, side, :, own_g:] = jnp.dot(
                pick, sib_s[...], preferred_element_type=f32).astype(bf16)

    low = lax.broadcasted_iota(jnp.int32, (8, 128), 0) < 4

    def products(k, side, dst, add):
        def quad(j, carry):
            first = k * span + j * 4
            r = [jnp.dot(sp[i % 2, side], chol2[first + i], preferred_element_type=f32)
                 for i in range(4)]
            at = pl.ds(pl.multiple_of(j * 48, 48), 48)
            for d in range(planes):
                pieces = []
                mixed = slice(planes * 8 + (d // 2) * 8, planes * 8 + (d // 2) * 8 + 8)
                for i in (0, 2):
                    even, odd = r[i][mixed], r[i + 1][mixed]
                    pieces += [r[i][d * 8:d * 8 + 8], r[i + 1][d * 8:d * 8 + 8],
                               jnp.where(low, even, odd) if d % 2 == 0 else jnp.where(low, odd, even)]
                value = jnp.concatenate(pieces, axis=0)
                if add:
                    value = value + dst[k, d, at].astype(f32)
                dst[k, d, at] = value.astype(bf16)
            return carry

        lax.fori_loop(0, span // 4, quad, 0)

    def hop(k, d, buf, send, recv, has_source, target):
        @pl.when(has_source)
        def _():
            remote(buf.at[k, d], buf.at[k, d], send.at[k, d], recv.at[k, d], target).wait_recv()
            buf[k, d] = (buf[k, d].astype(f32) + held[k, d].astype(f32)).astype(bf16)
            remote(buf.at[k, d], buf.at[k, d], send.at[k, d], recv.at[k, d], target).start()

        @pl.when(jnp.logical_not(has_source))
        def _():
            remote(held.at[k, d], buf.at[k, d], send.at[k, d], recv.at[k, d], target).start()

    def step(t, carry):
        @pl.when(t < chunks)
        def _():
            chol_load(t).wait()
            chol_swap(t).wait_recv()
            products(t, 1 - y, ysend, False)
            y_copy(t).start()

        @pl.when(jnp.logical_and(t >= 1, t <= chunks))
        def _():
            k = t - 1
            y_copy(k).wait_recv()
            products(k, y, held, True)

        ku = t - 1 - z

        @pl.when(jnp.logical_and(ku >= 0, ku < chunks))
        def _():
            for d in range(1, planes):
                @pl.when(d > z)
                def _():
                    hop(ku, d, up, up_send, up_recv, not_first, above)

        kd = t - planes + z

        @pl.when(jnp.logical_and(kd >= 0, kd < chunks))
        def _():
            for d in range(planes - 1):
                @pl.when(d < z)
                def _():
                    hop(kd, d, down, down_send, down_recv, not_last, below)

        kf = t - planes

        @pl.when(jnp.logical_and(kf >= 0, kf < chunks))
        def _():
            at = pl.ds(pl.multiple_of(kf * rows, 16), rows)

            @pl.when(jnp.logical_not(not_first))
            def _():
                remote(down.at[kf, z], down.at[kf, z], down_send.at[kf, z], down_recv.at[kf, z], above).wait_recv()
                out_ref[core, at] = (held[kf, z].astype(f32) + down[kf, z].astype(f32)).astype(bf16)

            @pl.when(jnp.logical_not(not_last))
            def _():
                remote(up.at[kf, z], up.at[kf, z], up_send.at[kf, z], up_recv.at[kf, z], below).wait_recv()
                out_ref[core, at] = (held[kf, z].astype(f32) + up[kf, z].astype(f32)).astype(bf16)

            @pl.when(jnp.logical_and(not_first, not_last))
            def _():
                remote(down.at[kf, z], down.at[kf, z], down_send.at[kf, z], down_recv.at[kf, z], above).wait_recv()
                remote(up.at[kf, z], up.at[kf, z], up_send.at[kf, z], up_recv.at[kf, z], below).wait_recv()
                out_ref[core, at] = (
                    held[kf, z].astype(f32) + up[kf, z].astype(f32) + down[kf, z].astype(f32)
                ).astype(bf16)

            out_copy(kf).start()

        return carry

    lax.fori_loop(0, chunks + planes, step, 0)

    def finish(k, carry):
        chol_swap(k).wait_send()
        y_copy(k).wait_send()
        for d in range(planes):
            @pl.when(d > z)
            def _():
                remote(up.at[k, d], up.at[k, d], up_send.at[k, d], up_recv.at[k, d], above).wait_send()

            @pl.when(d < z)
            def _():
                remote(down.at[k, d], down.at[k, d], down_send.at[k, d], down_recv.at[k, d], below).wait_send()

        out_copy(k).wait_send()
        other = out_ref.at[1 - core, pl.ds(pl.multiple_of(k * rows, 16), rows)]
        remote(other, other, out_send.at[k], out_recv.at[k], sibling).wait_recv()
        return carry

    lax.fori_loop(0, chunks, finish, 0)


def reduced_potential(shifted, chol_t, planes, chunks=16):
    n_walkers, own_g = shifted.shape
    norb = chol_t.shape[0]
    rows = norb // chunks * 12
    slots = pltpu.VMEM((chunks, planes, rows, 128), bf16)
    dma = pltpu.SemaphoreType.DMA
    return pl.pallas_call(
        functools.partial(scatter_kernel, planes, chunks),
        out_shape=jax.ShapeDtypeStruct((2, norb * 12, 128), bf16),
        in_specs=[pl.BlockSpec(memory_space=pltpu.VMEM), pl.BlockSpec(memory_space=pltpu.VMEM),
                  pl.BlockSpec(memory_space=pl.ANY)],
        out_specs=pl.BlockSpec(memory_space=pltpu.VMEM),
        scratch_shapes=[
            pltpu.VMEM((n_walkers, own_g), bf16),
            pltpu.VMEM((2, 2, n_walkers // 2, 2 * own_g), bf16),
            pltpu.VMEM((norb, 2 * own_g, 128), bf16),
            slots, slots, slots, slots,
            dma((2,)), dma((chunks,)), dma((chunks,)), dma((chunks,)), dma((chunks,)), dma((chunks,)),
            dma((chunks, planes)), dma((chunks, planes)), dma((chunks, planes)), dma((chunks, planes)),
            dma((chunks,)), dma((chunks,)),
        ],
        compiler_params=pltpu.CompilerParams(
            collective_id=0, has_side_effects=True, vmem_limit_bytes=58 * 2 ** 20),
        cost_estimate=pl.CostEstimate(
            flops=2 * n_walkers * norb * 256 * own_g, bytes_accessed=norb * own_g * 512, transcendentals=0),
    )(shifted, jnp.asarray(row_orders(planes), bf16), chol_t)


def body(planes, walkers, inv_intersection, trial_orbs, cholesky, aux_fields):
    me = lax.axis_index("blk")
    core, z = me % 2, me // 4
    rotated = jnp.einsum(
        "wpi,wij->wpj", walkers, inv_intersection, preferred_element_type=f32
    ).astype(bf16)
    own_half = jnp.einsum("pi,gpq->giq", trial_orbs, cholesky, preferred_element_type=f32).astype(bf16)
    everyone = lax.all_gather(rotated, "blk", axis=0, tiled=True)
    chol_t = jnp.transpose(cholesky, (1, 0, 2))
    force_bias = jnp.einsum("giq,wqi->wg", own_half, everyone, preferred_element_type=f32)
    shifted = (aux_fields + bias_step * force_bias).astype(bf16)
    norb = walkers.shape[1]
    summed = reduced_potential(shifted, chol_t, planes)
    summed = summed.reshape(2, norb // 2, 24, 128)
    straight = summed[:, :, :16].reshape(2, norb, 8, 128)
    mixed = summed[:, :, 16:].reshape(2, norb // 2, 2, 4, 128)
    mixed = jnp.where(z % 2 == 1, mixed[:, :, ::-1], mixed).reshape(2, norb, 4, 128)
    mine = jnp.where(core == 0, straight[:, :, :6],
                     jnp.concatenate([straight[:, :, 6:], mixed], axis=2))
    potential = jnp.transpose((root_step * mine.astype(f32)).astype(bf16), (2, 1, 0, 3))
    potential = potential.reshape(6, norb, norb)
    taylor_term = walkers
    total = walkers.astype(f32)
    for degree in range(1, 5):
        product = jnp.einsum("wpq,wqi->wpi", potential, taylor_term, preferred_element_type=f32)
        taylor_term = (product / degree).astype(bf16)
        total = total + taylor_term.astype(f32)
    new_walkers = total.astype(bf16)
    intersection = jnp.einsum("pi,wpj->wij", trial_orbs, new_walkers, preferred_element_type=f32)
    return (new_walkers, intersection)


def solution(mesh):
    planes = mesh.shape["blk"] // 4
    return jax.shard_map(
        functools.partial(body, planes),
        mesh=mesh,
        in_specs=(
            P(("groups", "blk"), None, None),
            P(("groups", "blk"), None, None),
            P(),
            P(("groups", "blk"), None, None),
            P("groups", "blk"),
        ),
        out_specs=(P(("groups", "blk"), None, None), P(("groups", "blk"), None, None)),
        check_vma=False,
    )
```

time: 274 us -> 200 us (0.73)
  waiting for transfers between devices: 172 us -> 21.2 us
  Pallas kernels: 0 us -> 90.3 us
  matrix products: 50.2 us -> 26 us
  local copies, waits for them, and re-layouts: 36.3 us -> 45.4 us
    reduce_scatter x1 -> x0, waiting for transfers between devices: 134 us -> none  [body(): lax.psum_scatter(terms.astype(jnp.bfloat16), 'blk', scatter_dimension=0,...]
    pallas_call x0 -> x1, Pallas kernels: none -> 90.3 us  [reduced_potential(): pl.pallas_call(functools.partial(scatter_kernel, planes, chunks), out_sha...]
    convert_element_type x2 -> x0, local copies, waits for them, and re-layouts: 25.5 us -> none  [the longest x1 13 us: body(): jnp.einsum('pi,gpq->giq', trial_orbs, cholesky, preferred_element_type=f32)]
    dot_general x1 -> x0, matrix products: 21 us -> none  [body(): jnp.einsum('wg,gpq->wpq', shifted, cholesky, preferred_element_type=f32)]
    unnamed x13 -> x15, local copies, waits for them, and re-layouts: 1.82 us -> 20.1 us
    all_gather x1, waiting for transfers between devices: 38.7 us -> 21.2 us  [body(): everyone = lax.all_gather(rotated, 'blk', axis=0, tiled=True)]
    dot_general x0 -> x1, local copies, waits for them, and re-layouts: none -> 12.3 us  [body(): jnp.einsum('pi,gpq->giq', trial_orbs, cholesky, preferred_element_type=f32)]
    dot_general x4, matrix products: 6.06 us -> 1.47 us  [body(): jnp.einsum('wpq,wqi->wpi', potential, taylor_term, preferred_element_type...]
  transfers between devices with their start and end apart: 2 -> 1, of which waited for: 2 -> 1; matrix products, arithmetic and copies ran while one was open for 10% -> 22% of each run, Pallas kernels for 0% -> 0%
where the time goes in v1:
time: 200 us; the launch traced here: 199 us
  Pallas kernels  90.3 us (45%)
  local copies, waits for them, and re-layouts  45.4 us (23%)
  matrix products  26 us (13%)
  waiting for transfers between devices  21.2 us (11%)
  between operations  14.2 us (7%)
    pallas_call x1, Pallas kernels, reduced_potential(): pl.pallas_call(functools.partial(scatter_kernel, planes, chunks), out_sha...  90.3 us
    all_gather x1, waiting for transfers between devices, body(): everyone = lax.all_gather(rotated, 'blk', axis=0, tiled=True)  21.2 us
    unnamed x15, local copies, waits for them, and re-layouts  20.1 us
    dot_general x1, matrix products, body(): jnp.einsum('pi,gpq->giq', trial_orbs, cholesky, preferred_element_type=f32)  13.7 us
    dot_general x1, local copies, waits for them, and re-layouts, body(): jnp.einsum('pi,gpq->giq', trial_orbs, cholesky, preferred_element_type=f32)  12.3 us
    all_gather x1, local copies, waits for them, and re-layouts, body(): everyone = lax.all_gather(rotated, 'blk', axis=0, tiled=True)  9.05 us
    dot_general x1, matrix products, body(): jnp.einsum('giq,wqi->wg', own_half, everyone, preferred_element_type=f32)  8.55 us
  transfers between devices with their start and end apart: 1, of which 1 were waited for; matrix products, arithmetic and copies ran while one was open for 22% of the time, Pallas kernels for 0%

profile of v1, /device:TPU:0, one launch (start us, length us, event | category | flops | bytes accessed | tf_op | source)
XLA Modules:
  0.0 199.0 jit_solution(11119086032100547271)
XLA Ops:
  7.2 0.0 all-gather.2.cloned.1.call-start
  7.2 0.9 copy-done
  8.1 2.0 %convolution_convert_fusion.1 = bf16[6,256,128]{2,1,0:T(8,128)(2,1)} fusion(bf16[6,256,128]{2,1,0:T(8,128)(2,1)} %param.6, bf16[6,128,128]{2,1,0:T(8,128)(2,1)S(1)} %copy-done), kind=kOutput, calls=%fused_computation.15 | convolution fusion | flops 50528256 | bytes 983040 | tf_op jit(solution)/shard_map/wpi,wij->wpj/dot_general | solution.py:256
  10.2 18.0 %copy.27 = bf16[128,256,256]{2,0,1:T(8,128)(2,1)} copy(bf16[128,256,256]{2,1,0:T(8,128)(2,1)} %param.9) | data formatting | bytes 33554432 | tf_op args[3]
  28.2 13.7 %fusion.23 = bf16[128,256,128]{2,1,0:T(8,128)(2,1)} fusion(bf16[128,256,256]{2,1,0:T(8,128)(2,1)} %param.9, bf16[256,128]{1,0:T(8,128)(2,1)S(1)} %copy-done.4), kind=kOutput, calls=%fused_computation.25 | convolution fusion | flops 2147483648 | bytes 25231360 | tf_op jit(solution)/shard_map/pi,gpq->giq/dot_general | solution.py:259
  41.9 12.3 %copy.21 = bf16[128,256,128]{1,0,2:T(8,128)(2,1)} copy(bf16[128,256,128]{2,1,0:T(8,128)(2,1)} %fusion.23) | data formatting | bytes 16777216 | tf_op jit(solution)/shard_map/pi,gpq->giq/dot_general | solution.py:259
  54.2 21.2 %all-gather.2.cloned.1.call-done = bf16[96,256,128]{2,1,0:T(8,128)(2,1)} async-done(((bf16[6,256,128]{2,1,0:T(8,128)(2,1)}), bf16[96,256,128]{2,1,0:T(8,128)(2,1)}) %all-gather.2.cloned.1.call-update) | async-done | bytes 6291472 | tf_op jit(solution)/shard_map/all_gather | solution.py:260
  75.5 9.1 %copy.14 = bf16[96,256,128]{1,0,2:T(8,128)(2,1)} copy(bf16[96,256,128]{2,1,0:T(8,128)(2,1)} %all-gather.2.cloned.1.call-done) | data formatting | bytes 12582912 | tf_op jit(solution)/shard_map/all_gather | solution.py:260
  84.5 8.6 %fusion.18.s_ref = bf16[96,128]{1,0:T(8,128)(2,1)} fusion(f32[96,128]{1,0:T(8,128)S(1)} %copy-done.5, bf16[96,256,128]{1,0,2:T(8,128)(2,1)} %copy.14, bf16[128,256,128]{1,0,2:T(8,128)(2,1)} %copy.21), kind=kOutput, calls=%fused_computation.21 | convolution fusion | flops 805343232 | bytes 14753792 | tf_op jit(solution)/shard_map/giq,wqi->wg/dot_general | solution.py:262
  93.1 90.3 %shard_map.77 = bf16[2,3072,128]{2,1,0:T(8,128)(2,1)} custom-call(bf16[96,128]{1,0:T(8,128)(2,1)} %fusion.18.s_ref, bf16[192,96]{1,0:T(8,128)(2,1)} %constant.51.clone.perm_ref, bf16[256,128,256]{2,1,0:T(8,128)(2,1)} %bitcast.49), custom_call_target="tpu_custom_call" | custom-call | flops 1610612736 | bytes 16777216 | tf_op jit(solution)/shard_map/pallas_call | solution.py:231
  183.4 1.1 slice.19
  184.6 1.4 slice.16
  186.0 0.3 reverse_select_fusion
  186.3 0.5 copy.18
  186.8 0.3 slice.18
  187.1 0.3 copy.24
  187.4 1.5 fusion.21
  188.9 0.5 reshape.23
  189.4 0.4 convolution_convert_fusion
  189.7 0.4 fusion.3
  190.1 0.4 fusion.4
  190.5 0.4 fusion.8
  190.9 0.3 convolution_bitcast_fusion
  191.2 0.9 copy.20
  (12 shorter events, 0.1 us)
Async XLA Ops:
  7.2 0.9 copy-start
  7.2 68.3 %all-gather.2.cloned.1.call-start = ((), (), s32[]{:S(2)}) async-start(), calls=%async_computation | async-start | bytes 6684672 | tf_op jit(solution)/shard_map/all_gather | solution.py:260
  10.2 18.1 %copy-start.4 = (bf16[256,128]{1,0:T(8,128)(2,1)S(1)}, bf16[256,128]{1,0:T(8,128)(2,1)}, u32[]{:S(2)}) copy-start(bf16[256,128]{1,0:T(8,128)(2,1)} %param.8) | copy-start | bytes 196612
  54.2 30.3 %copy-start.5 = (f32[96,128]{1,0:T(8,128)S(1)}, f32[96,128]{1,0:T(8,128)}, u32[]{:S(2)}) copy-start(f32[96,128]{1,0:T(8,128)} %param.10) | copy-start | bytes 147460
  183.4 6.0 %copy-start.2 = (bf16[6,256,128]{2,1,0:T(8,128)(2,1)S(1)}, bf16[6,256,128]{2,1,0:T(8,128)(2,1)}, u32[]{:S(2)}) copy-start(bf16[6,256,128]{2,1,0:T(8,128)(2,1)} %param.6) | copy-start | bytes 1179652
  184.5 7.6 %copy-start.1 = (bf16[6,128,128]{2,1,0:T(8,128)(2,1)S(1)}, bf16[6,128,128]{2,1,0:T(8,128)(2,1)}, u32[]{:S(2)}) copy-start(bf16[6,128,128]{2,1,0:T(8,128)(2,1)} %param.7) | copy-start | bytes 589828
  190.9 1.2 copy-start.3
Sparse Core Ops, SparseCore 0:
  10.9 64.5 all-gather.1

commit v2 on v1

--- a/solution.py
+++ b/solution.py
@@ -33,10 +33,10 @@
 
 
 def scatter_kernel(planes, chunks, s_ref, perm_ref, chol_ref, out_ref,
-                   sib_s, sp, chol2, ysend, held, up, down,
+                   sib_s, sp, raw, turned, ysend, held, up, down,
                    s_sem, load_sem, chol_send, chol_recv, y_send, y_recv,
                    up_send, up_recv, down_send, down_recv, out_send, out_recv):
-    norb, own_g, _ = chol_ref.shape
+    own_g, norb, _ = chol_ref.shape
     span = norb // chunks
     rows = span * 12
     half = planes * 12
@@ -72,13 +72,15 @@
 
     def chol_load(k):
         return pltpu.make_async_copy(
-            chol_ref.at[pl.ds(k * span, span), :, pl.ds(pl.multiple_of(core * 128, 128), 128)],
-            chol2.at[pl.ds(k * span, span), pl.ds(0, own_g)], load_sem.at[k])
+            chol_ref.at[:, pl.ds(pl.multiple_of(k * span, span), span),
+                        pl.ds(pl.multiple_of(core * 128, 128), 128)],
+            raw.at[pl.ds(0, own_g), pl.ds(pl.multiple_of(k * span, span), span)], load_sem.at[k])
 
     def chol_swap(k):
         return remote(
-            chol_ref.at[pl.ds(k * span, span), :, pl.ds(pl.multiple_of((1 - core) * 128, 128), 128)],
-            chol2.at[pl.ds(k * span, span), pl.ds(own_g, own_g)],
+            chol_ref.at[:, pl.ds(pl.multiple_of(k * span, span), span),
+                        pl.ds(pl.multiple_of((1 - core) * 128, 128), 128)],
+            raw.at[pl.ds(own_g, own_g), pl.ds(pl.multiple_of(k * span, span), span)],
             chol_send.at[k], chol_recv.at[k], sibling)
 
     def y_copy(k):
@@ -110,8 +112,8 @@
 
     def products(k, side, dst, add):
         def quad(j, carry):
-            first = k * span + j * 4
-            r = [jnp.dot(sp[i % 2, side], chol2[first + i], preferred_element_type=f32)
+            slot = lax.rem(k, 2)
+            r = [jnp.dot(sp[i % 2, side], turned[slot, j * 4 + i], preferred_element_type=f32)
                  for i in range(4)]
             at = pl.ds(pl.multiple_of(j * 48, 48), 48)
             for d in range(planes):
@@ -145,6 +147,14 @@
         def _():
             chol_load(t).wait()
             chol_swap(t).wait_recv()
+            columns = pl.ds(pl.multiple_of(t * span, span), span)
+
+            def turn(b, carry):
+                at = pl.ds(pl.multiple_of(b * 16, 16), 16)
+                turned[lax.rem(t, 2), :, at, :] = jnp.swapaxes(raw[at, columns, :], 0, 1)
+                return carry
+
+            lax.fori_loop(0, 2 * own_g // 16, turn, 0)
             products(t, 1 - y, ysend, False)
             y_copy(t).start()
 
@@ -222,9 +232,9 @@
     lax.fori_loop(0, chunks, finish, 0)
 
 
-def reduced_potential(shifted, chol_t, planes, chunks=16):
+def reduced_potential(shifted, cholesky, planes, chunks=16):
     n_walkers, own_g = shifted.shape
-    norb = chol_t.shape[0]
+    norb = cholesky.shape[1]
     rows = norb // chunks * 12
     slots = pltpu.VMEM((chunks, planes, rows, 128), bf16)
     dma = pltpu.SemaphoreType.DMA
@@ -237,7 +247,8 @@
         scratch_shapes=[
             pltpu.VMEM((n_walkers, own_g), bf16),
             pltpu.VMEM((2, 2, n_walkers // 2, 2 * own_g), bf16),
-            pltpu.VMEM((norb, 2 * own_g, 128), bf16),
+            pltpu.VMEM((2 * own_g, norb, 128), bf16),
+            pltpu.VMEM((2, norb // chunks, 2 * own_g, 128), bf16),
             slots, slots, slots, slots,
             dma((2,)), dma((chunks,)), dma((chunks,)), dma((chunks,)), dma((chunks,)), dma((chunks,)),
             dma((chunks, planes)), dma((chunks, planes)), dma((chunks, planes)), dma((chunks, planes)),
@@ -247,26 +258,34 @@
             collective_id=0, has_side_effects=True, vmem_limit_bytes=58 * 2 ** 20),
         cost_estimate=pl.CostEstimate(
             flops=2 * n_walkers * norb * 256 * own_g, bytes_accessed=norb * own_g * 512, transcendentals=0),
-    )(shifted, jnp.asarray(row_orders(planes), bf16), chol_t)
+    )(shifted, jnp.asarray(row_orders(planes), bf16), cholesky)
 
 
 def body(planes, walkers, inv_intersection, trial_orbs, cholesky, aux_fields):
     me = lax.axis_index("blk")
-    core, z = me % 2, me // 4
+    core, z = lax.rem(me, 2), lax.div(me, 4)
     rotated = jnp.einsum(
         "wpi,wij->wpj", walkers, inv_intersection, preferred_element_type=f32
     ).astype(bf16)
     own_half = jnp.einsum("pi,gpq->giq", trial_orbs, cholesky, preferred_element_type=f32).astype(bf16)
-    everyone = lax.all_gather(rotated, "blk", axis=0, tiled=True)
-    chol_t = jnp.transpose(cholesky, (1, 0, 2))
-    force_bias = jnp.einsum("giq,wqi->wg", own_half, everyone, preferred_element_type=f32)
+    n_dev = planes * 4
+    same_core = lax.all_gather(
+        rotated, "blk", axis=0, tiled=True,
+        axis_index_groups=[list(range(0, n_dev, 2)), list(range(1, n_dev, 2))])
+    same_core, own_half = lax.optimization_barrier((same_core, own_half))
+    other_core = lax.ppermute(same_core, "blk", [(i, i ^ 1) for i in range(n_dev)])
+    biases = [jnp.einsum("giq,wqi->wg", own_half, some, preferred_element_type=f32)
+              for some in (same_core, other_core)]
+    biases = [b.reshape(n_dev // 2, 1, -1, b.shape[1]) for b in biases]
+    force_bias = jnp.where(core == 0, jnp.concatenate(biases, axis=1),
+                           jnp.concatenate(biases[::-1], axis=1)).reshape(aux_fields.shape)
     shifted = (aux_fields + bias_step * force_bias).astype(bf16)
     norb = walkers.shape[1]
-    summed = reduced_potential(shifted, chol_t, planes)
+    summed = reduced_potential(shifted, cholesky, planes)
     summed = summed.reshape(2, norb // 2, 24, 128)
     straight = summed[:, :, :16].reshape(2, norb, 8, 128)
     mixed = summed[:, :, 16:].reshape(2, norb // 2, 2, 4, 128)
-    mixed = jnp.where(z % 2 == 1, mixed[:, :, ::-1], mixed).reshape(2, norb, 4, 128)
+    mixed = jnp.where(lax.rem(z, 2) == 1, mixed[:, :, ::-1], mixed).reshape(2, norb, 4, 128)
     mine = jnp.where(core == 0, straight[:, :, :6],
                      jnp.concatenate([straight[:, :, 6:], mixed], axis=2))
     potential = jnp.transpose((root_step * mine.astype(f32)).astype(bf16), (2, 1, 0, 3))

time: 200 us -> 212 us (1.060)
  waiting for transfers between devices: 21.2 us -> 50.3 us
  local copies, waits for them, and re-layouts: 45.4 us -> 22.3 us
  matrix products: 26 us -> 30.7 us
    all_gather x1, waiting for transfers between devices: 21.2 us -> 50.2 us  [body(): lax.all_gather(rotated, 'blk', axis=0, tiled=True, axis_index_groups=[lis...]
    unnamed x15 -> x12, local copies, waits for them, and re-layouts: 20.1 us -> 2.09 us
    optimization_barrier x0 -> x2, local copies, waits for them, and re-layouts: none -> 16.2 us  [body(): same_core, own_half = lax.optimization_barrier((same_core, own_half))]
    dot_general x1 -> x0, local copies, waits for them, and re-layouts: 12.3 us -> none  [body(): jnp.einsum('pi,gpq->giq', trial_orbs, cholesky, preferred_element_type=f32)]
    all_gather x1 -> x0, local copies, waits for them, and re-layouts: 9.05 us -> none  [body(): everyone = lax.all_gather(rotated, 'blk', axis=0, tiled=True)]
    dot_general x1 -> x2, matrix products: 8.55 us -> 13.3 us  [body(): jnp.einsum('giq,wqi->wg', own_half, some, preferred_element_type=f32)]
  transfers between devices with their start and end apart: 1 -> 2, of which waited for: 1 -> 1; matrix products, arithmetic and copies ran while one was open for 22% -> 15% of each run, Pallas kernels for 0% -> 0%
where the time goes in v2:
time: 212 us; the launch traced here: 211 us
  Pallas kernels  90.9 us (43%)
  waiting for transfers between devices  50.3 us (24%)
  matrix products  30.7 us (14%)
  local copies, waits for them, and re-layouts  22.3 us (11%)
  between operations  14.3 us (7%)
  other arithmetic  2.36 us (1%)
    pallas_call x1, Pallas kernels, reduced_potential(): pl.pallas_call(functools.partial(scatter_kernel, planes, chunks), out_sha...  90.9 us
    all_gather x1, waiting for transfers between devices, body(): lax.all_gather(rotated, 'blk', axis=0, tiled=True, axis_index_groups=[lis...  50.2 us
    optimization_barrier x2, local copies, waits for them, and re-layouts, body(): same_core, own_half = lax.optimization_barrier((same_core, own_half))  16.2 us
    dot_general x1, matrix products, body(): jnp.einsum('pi,gpq->giq', trial_orbs, cholesky, preferred_element_type=f32)  13.6 us
    dot_general x2, matrix products, body(): jnp.einsum('giq,wqi->wg', own_half, some, preferred_element_type=f32)  13.3 us
  transfers between devices with their start and end apart: 2, of which 1 were waited for; matrix products, arithmetic and copies ran while one was open for 15% of the time, Pallas kernels for 0%

profile of v2, /device:TPU:0, one launch (start us, length us, event | category | flops | bytes accessed | tf_op | source)
XLA Modules:
  0.0 210.9 jit_solution(16108423858058694946)
XLA Ops:
  7.2 0.9 copy-done
  8.1 2.0 convolution_convert_fusion.1
  10.1 13.6 %convert_bitcast_fusion = bf16[128,128,256]{1,2,0:T(8,128)(2,1)} fusion(bf16[128,256,256]{2,1,0:T(8,128)(2,1)} %chol_ref.1, bf16[256,128]{1,0:T(8,128)(2,1)} %param.8), kind=kOutput, calls=%fused_computation | convolution fusion | flops 2151677952 | bytes 25231360 | tf_op jit(solution)/shard_map/pi,gpq->giq/dot_general | solution.py:270
  23.7 50.2 %all-gather.2.cloned.1.call-done = bf16[48,256,128]{2,1,0:T(8,128)(2,1)} async-done(((bf16[6,256,128]{2,1,0:T(8,128)(2,1)}), bf16[48,256,128]{2,1,0:T(8,128)(2,1)}) %all-gather.2.cloned.1.call-update) | async-done | bytes 3145744 | tf_op jit(solution)/shard_map/all_gather | solution.py:272
  74.0 3.8 %copy.45 = bf16[48,256,128]{1,0,2:T(8,128)(2,1)S(1)} copy(bf16[48,256,128]{2,1,0:T(8,128)(2,1)} %all-gather.2.cloned.1.call-done) | data formatting | bytes 6291456 | tf_op jit(solution)/shard_map/optimization_barrier | solution.py:275
  77.9 12.4 %copy.46 = bf16[128,128,256]{2,0,1:T(8,128)(2,1)} copy(bf16[128,128,256]{1,2,0:T(8,128)(2,1)} %convert_bitcast_fusion) | data formatting | bytes 16777216 | tf_op jit(solution)/shard_map/optimization_barrier | solution.py:275
  90.3 6.2 %convolution_bitcast_fusion.2 = f32[48,128]{1,0:T(8,128)S(1)} fusion(bf16[48,256,128]{1,0,2:T(8,128)(2,1)S(1)} %copy.45, bf16[128,128,256]{2,0,1:T(8,128)(2,1)} %copy.46), kind=kOutput, calls=%fused_computation.16 | convolution fusion | flops 402653184 | bytes 11558912 | tf_op jit(solution)/shard_map/giq,wqi->wg/dot_general | solution.py:277
  96.6 7.2 %convolution_bitcast_fusion.1 = f32[48,128]{1,0:T(8,128)S(1)} fusion(bf16[48,256,128]{1,0,2:T(8,128)(2,1)} %collective-permute-done, bf16[128,128,256]{2,0,1:T(8,128)(2,1)} %copy.46), kind=kOutput, calls=%fused_computation.15 | convolution fusion | flops 402653184 | bytes 11558912 | tf_op jit(solution)/shard_map/giq,wqi->wg/dot_general | solution.py:277
  103.8 0.6 add_convert_fusion.s_ref
  104.4 90.9 %shard_map.77 = bf16[2,3072,128]{2,1,0:T(8,128)(2,1)} custom-call(bf16[96,128]{1,0:T(8,128)(2,1)} %add_convert_fusion.s_ref, bf16[192,96]{1,0:T(8,128)(2,1)} %constant.32.clone.perm_ref, bf16[128,256,256]{2,1,0:T(8,128)(2,1)} %chol_ref.1), custom_call_target="tpu_custom_call" | custom-call | flops 1610612736 | bytes 16777216 | tf_op jit(solution)/shard_map/pallas_call | solution.py:241
  195.3 1.1 slice.19
  196.5 1.4 slice.16
  197.9 0.3 reverse_select_fusion
  198.2 0.5 copy.56
  198.7 0.3 slice.18
  199.0 0.3 copy.62
  199.3 1.5 fusion.6
  200.8 0.5 reshape.38
  201.3 0.4 convolution_convert_fusion
  201.7 0.4 fusion
  202.0 0.4 fusion.1
  202.4 0.4 fusion.5
  202.8 0.3 convolution_bitcast_fusion
  203.1 0.9 copy.58
  (20 shorter events, 0.2 us)
Async XLA Ops:
  7.2 0.9 copy-start
  7.2 66.8 %all-gather.2.cloned.1.call-start = ((), (), s32[]{:S(2)}) async-start(), calls=%async_computation | async-start | bytes 3538944 | tf_op jit(solution)/shard_map/all_gather | solution.py:272
  77.8 18.7 %collective-permute-start = (bf16[48,256,128]{1,0,2:T(8,128)(2,1)S(1)}, bf16[48,256,128]{1,0,2:T(8,128)(2,1)}, u32[]{:S(2)}, u32[]{:S(2)}) collective-permute-start(bf16[48,256,128]{1,0,2:T(8,128)(2,1)S(1)} %copy.45), channel_id=1, source_target_pairs={{0,1},{1,0},{2,3},{3,2},{4,5},{5,4},{6,7},{7,6},{8,9},{9,8},{10,11... | collective-permute-start | bytes 9437192 | tf_op jit(solution)/shard_map/ppermute | solution.py:276
  96.5 7.3 %copy-start.4 = (f32[96,128]{1,0:T(8,128)S(1)}, f32[96,128]{1,0:T(8,128)}, u32[]{:S(2)}) copy-start(f32[96,128]{1,0:T(8,128)} %param.10) | copy-start | bytes 147460
  195.3 6.0 %copy-start.1 = (bf16[6,256,128]{2,1,0:T(8,128)(2,1)S(1)}, bf16[6,256,128]{2,1,0:T(8,128)(2,1)}, u32[]{:S(2)}) copy-start(bf16[6,256,128]{2,1,0:T(8,128)(2,1)} %param.6) | copy-start | bytes 1179652
  196.5 6.3 %copy-start.3 = (bf16[256,128]{1,0:T(8,128)(2,1)S(1)}, bf16[256,128]{1,0:T(8,128)(2,1)}, u32[]{:S(2)}) copy-start(bf16[256,128]{1,0:T(8,128)(2,1)} %param.8) | copy-start | bytes 196612
  202.8 1.2 copy-start.2
Sparse Core Ops, SparseCore 0:
  10.8 63.1 all-gather.1

commit v3 on v2

--- a/solution.py
+++ b/solution.py
@@ -261,25 +261,221 @@
     )(shifted, jnp.asarray(row_orders(planes), bf16), cholesky)
 
 
+def bias_kernel(planes, rot_ref, trial_ref, chol_ref, aux_ref, out_ref,
+                chol, part, half_rot, gathered, turned,
+                load_sem, own_sem, z_recv, up_send, down_send, y_send, y_recv, sib_send, sib_recv):
+    own_g, norb, _ = chol_ref.shape
+    count, nocc, _ = rot_ref.shape
+    n_walkers = gathered.shape[0]
+    blocks = own_g // 16
+    me = lax.axis_index("blk")
+    core = lax.rem(me, 2)
+    y = lax.rem(lax.div(me, 2), 2)
+    z = lax.div(me, 4)
+    sibling = me + 1 - 2 * core
+    across = me + 2 - 4 * y
+    above = me + 4
+    below = me - 4
+    not_first, not_last = z > 0, z < planes - 1
+
+    def load(b):
+        at = pl.ds(b * 16, 16)
+        return pltpu.make_async_copy(chol_ref.at[at], chol.at[at], load_sem.at[b])
+
+    for b in range(blocks):
+        load(b).start()
+
+    barrier = pltpu.get_barrier_semaphore()
+    pl.semaphore_signal(barrier, inc=1, device_id={"blk": sibling}, device_id_type=MESH)
+    pl.semaphore_signal(barrier, inc=1, device_id={"blk": across}, device_id_type=MESH)
+
+    @pl.when(not_first)
+    def _():
+        pl.semaphore_signal(barrier, inc=1, device_id={"blk": below}, device_id_type=MESH)
+
+    @pl.when(not_last)
+    def _():
+        pl.semaphore_signal(barrier, inc=1, device_id={"blk": above}, device_id_type=MESH)
+
+    peers = 2 + jnp.where(not_first, 1, 0) + jnp.where(not_last, 1, 0)
+    pl.semaphore_wait(barrier, peers)
+
+    def move(plane, column, owner_core, send, recv, target):
+        piece = gathered.at[pl.ds(((plane * 2 + column) * 2 + owner_core) * count, count)]
+        return pltpu.make_async_remote_copy(
+            src_ref=piece, dst_ref=piece, send_sem=send, recv_sem=recv,
+            device_id={"blk": target}, device_id_type=MESH)
+
+    def go_up(plane):
+        return move(plane, y, core, up_send.at[plane], z_recv.at[plane], above)
+
+    def go_down(plane):
+        return move(plane, y, core, down_send.at[plane], z_recv.at[plane], below)
+
+    def go_across(plane):
+        return move(plane, y, core, y_send.at[plane], y_recv.at[plane], across)
+
+    def from_across(plane):
+        return move(plane, 1 - y, core, y_send.at[plane], y_recv.at[plane], across)
+
+    def go_sibling(plane, column):
+        return move(plane, column, core, sib_send.at[plane, column], sib_recv.at[plane, column], sibling)
+
+    def from_sibling(plane, column):
+        return move(plane, column, 1 - core, sib_send.at[plane, column], sib_recv.at[plane, column], sibling)
+
+    own = pltpu.make_async_copy(rot_ref, gathered.at[pl.ds(me * count, count)], own_sem)
+    own.start()
+    own.wait()
+
+    @pl.when(not_last)
+    def _():
+        go_up(z).start()
+
+    @pl.when(not_first)
+    def _():
+        go_down(z).start()
+
+    go_across(z).start()
+    go_sibling(z, y).start()
+
+    def make_half(b):
+        load(b).wait()
+
+        def one(j, carry):
+            part[j] = jnp.dot(trial_ref[...], chol[b * 16 + j], preferred_element_type=f32).astype(bf16)
+            return carry
+
+        lax.fori_loop(0, 16, one, 0)
+
+        def turn(i, carry):
+            at = pl.ds(pl.multiple_of(i * 16, 16), 16)
+            half_rot[at, pl.ds(b * 16, 16), :] = jnp.swapaxes(part[:, at, :], 0, 1)
+            return carry
+
+        lax.fori_loop(0, nocc // 16, turn, 0)
+
+    done = 0
+    for t in range(1, planes + 1):
+        until = -(-blocks * t // planes)
+        for b in range(done, until):
+            make_half(b)
+        done = until
+        if t < planes:
+            low, high = z - t, z + t
+
+            @pl.when(low >= 0)
+            def _():
+                go_up(low).wait_recv()
+
+                @pl.when(not_last)
+                def _():
+                    go_up(low).start()
+
+                go_across(low).start()
+                go_sibling(low, y).start()
+
+            @pl.when(high < planes)
+            def _():
+                go_down(high).wait_recv()
+
+                @pl.when(not_first)
+                def _():
+                    go_down(high).start()
+
+                go_across(high).start()
+                go_sibling(high, y).start()
+
+        def pass_on(plane):
+            from_across(plane).wait_recv()
+            go_sibling(plane, 1 - y).start()
+
+        if t == 1:
+            pass_on(z)
+        else:
+            @pl.when(z - (t - 1) >= 0)
+            def _():
+                pass_on(z - (t - 1))
+
+            @pl.when(z + (t - 1) < planes)
+            def _():
+                pass_on(z + (t - 1))
+
+    for plane in range(planes):
+        for column in range(2):
+            from_sibling(plane, column).wait_recv()
+
+    def turn_walkers(w, carry):
+        rows = pl.ds(pl.multiple_of(w * 16, 16), 16)
+
+        def turn(i, carry):
+            at = pl.ds(pl.multiple_of(i * 16, 16), 16)
+            turned[at, rows, :] = jnp.swapaxes(gathered[rows, at, :], 0, 1)
+            return carry
+
+        return lax.fori_loop(0, nocc // 16, turn, carry)
+
+    lax.fori_loop(0, n_walkers // 16, turn_walkers, 0)
+
+    def contract(i, total):
+        for j in range(4):
+            total = total + lax.dot_general(
+                turned[i * 4 + j], half_rot[i * 4 + j], (((1,), (1,)), ((), ())),
+                preferred_element_type=f32)
+        return total
+
+    bias = lax.fori_loop(0, nocc // 4, contract, jnp.zeros((n_walkers, own_g), f32))
+    out_ref[...] = (aux_ref[...] + bias_step * bias).astype(bf16)
+
+    for plane in range(planes):
+        @pl.when(jnp.logical_and(plane <= z, not_last))
+        def _():
+            go_up(plane).wait_send()
+
+        @pl.when(jnp.logical_and(plane >= z, not_first))
+        def _():
+            go_down(plane).wait_send()
+
+        go_across(plane).wait_send()
+        for column in range(2):
+            go_sibling(plane, column).wait_send()
+
+
+def shifted_fields(rotated, trial_t, cholesky, aux_fields, planes):
+    own_g, norb, _ = cholesky.shape
+    nocc = trial_t.shape[0]
+    n_walkers = aux_fields.shape[0]
+    vmem = pl.BlockSpec(memory_space=pltpu.VMEM)
+    dma = pltpu.SemaphoreType.DMA
+    return pl.pallas_call(
+        functools.partial(bias_kernel, planes),
+        out_shape=jax.ShapeDtypeStruct((n_walkers, own_g), bf16),
+        in_specs=[vmem, vmem, pl.BlockSpec(memory_space=pl.ANY), vmem],
+        out_specs=vmem,
+        scratch_shapes=[
+            pltpu.VMEM((own_g, norb, norb), bf16),
+            pltpu.VMEM((16, nocc, norb), bf16),
+            pltpu.VMEM((nocc, own_g, norb), bf16),
+            pltpu.VMEM((n_walkers, nocc, norb), bf16),
+            pltpu.VMEM((nocc, n_walkers, norb), bf16),
+            dma((own_g // 16,)), dma(()), dma((planes,)), dma((planes,)), dma((planes,)),
+            dma((planes,)), dma((planes,)), dma((planes, 2)), dma((planes, 2)),
+        ],
+        compiler_params=pltpu.CompilerParams(
+            collective_id=1, has_side_effects=True, vmem_limit_bytes=58 * 2 ** 20),
+        cost_estimate=pl.CostEstimate(
+            flops=2 * own_g * nocc * norb * (norb + n_walkers),
+            bytes_accessed=own_g * norb * norb * 2, transcendentals=0),
+    )(rotated, trial_t, cholesky, aux_fields)
+
+
 def body(planes, walkers, inv_intersection, trial_orbs, cholesky, aux_fields):
     me = lax.axis_index("blk")
     core, z = lax.rem(me, 2), lax.div(me, 4)
     rotated = jnp.einsum(
-        "wpi,wij->wpj", walkers, inv_intersection, preferred_element_type=f32
+        "wpi,wij->wjp", walkers, inv_intersection, preferred_element_type=f32
     ).astype(bf16)
-    own_half = jnp.einsum("pi,gpq->giq", trial_orbs, cholesky, preferred_element_type=f32).astype(bf16)
-    n_dev = planes * 4
-    same_core = lax.all_gather(
-        rotated, "blk", axis=0, tiled=True,
-        axis_index_groups=[list(range(0, n_dev, 2)), list(range(1, n_dev, 2))])
-    same_core, own_half = lax.optimization_barrier((same_core, own_half))
-    other_core = lax.ppermute(same_core, "blk", [(i, i ^ 1) for i in range(n_dev)])
-    biases = [jnp.einsum("giq,wqi->wg", own_half, some, preferred_element_type=f32)
-              for some in (same_core, other_core)]
-    biases = [b.reshape(n_dev // 2, 1, -1, b.shape[1]) for b in biases]
-    force_bias = jnp.where(core == 0, jnp.concatenate(biases, axis=1),
-                           jnp.concatenate(biases[::-1], axis=1)).reshape(aux_fields.shape)
-    shifted = (aux_fields + bias_step * force_bias).astype(bf16)
+    shifted = shifted_fields(rotated, trial_orbs.T, cholesky, aux_fields, planes)
     norb = walkers.shape[1]
     summed = reduced_potential(shifted, cholesky, planes)
     summed = summed.reshape(2, norb // 2, 24, 128)

time: 212 us -> 163 us (0.77)
  Pallas kernels: 90.9 us -> 150 us
  waiting for transfers between devices: 50.3 us -> 0 us
  matrix products: 30.7 us -> 3.82 us
  local copies, waits for them, and re-layouts: 22.3 us -> 6.8 us
  between operations: 14.3 us -> 0.81 us
    pallas_call x0 -> x1, Pallas kernels: none -> 53.2 us  [shifted_fields(): pl.pallas_call(functools.partial(bias_kernel, planes), out_shape=jax.Shap...]
    all_gather x1 -> x0, waiting for transfers between devices: 50.2 us -> none  [body(): lax.all_gather(rotated, 'blk', axis=0, tiled=True, axis_index_groups=[lis...]
    dot_general x4 -> x1, matrix products: 28.9 us -> 2.05 us  [body(): jnp.einsum('wpi,wij->wjp', walkers, inv_intersection, preferred_element_t...]
    optimization_barrier x2 -> x0, local copies, waits for them, and re-layouts: 16.2 us -> none  [body(): same_core, own_half = lax.optimization_barrier((same_core, own_half))]
    pallas_call x1, Pallas kernels: 90.9 us -> 96.4 us  [reduced_potential(): pl.pallas_call(functools.partial(scatter_kernel, planes, chunks), out_sha...]
  transfers between devices with their start and end apart: 2 -> 0, of which waited for: 1 -> 0; matrix products, arithmetic and copies ran while one was open for 15% -> 0% of each run, Pallas kernels for 0% -> 0%
where the time goes in v3:
time: 163 us
  Pallas kernels  150 us (92%)
  local copies, waits for them, and re-layouts  6.8 us (4%)
  matrix products  3.82 us (2%)
  other arithmetic  1.74 us (1%)
    pallas_call x1, Pallas kernels, reduced_potential(): pl.pallas_call(functools.partial(scatter_kernel, planes, chunks), out_sha...  96.4 us
    pallas_call x1, Pallas kernels, shifted_fields(): pl.pallas_call(functools.partial(bias_kernel, planes), out_shape=jax.Shap...  53.2 us
    unnamed x13, local copies, waits for them, and re-layouts  4.1 us

profile of v3, /device:TPU:0, one launch (start us, length us, event | category | flops | bytes accessed | tf_op | source)
XLA Modules:
  0.0 162.7 jit_solution(10562494226622528590)
XLA Ops:
  0.6 0.0 copy-start
  0.7 0.9 copy-done
  1.6 2.1 %convolution_convert_fusion.1.rot_ref = bf16[6,128,256]{2,1,0:T(8,128)(2,1)} fusion(bf16[6,128,128]{2,1,0:T(8,128)(2,1)S(1)} %copy-done, bf16[6,256,128]{2,1,0:T(8,128)(2,1)} %param.6), kind=kOutput, calls=%fused_computation.11 | convolution fusion | flops 50528256 | bytes 983040 | tf_op jit(solution)/shard_map/wpi,wij->wjp/dot_general | solution.py:475
  3.6 1.6 copy.9
  5.2 53.2 %shard_map.77.s_ref = bf16[96,128]{1,0:T(8,128)(2,1)} custom-call(bf16[6,128,256]{2,1,0:T(8,128)(2,1)} %convolution_convert_fusion.1.rot_ref, bf16[128,256]{1,0:T(8,128)(2,1)} %bitcast.30, bf16[128,256,256]{2,1,0:T(8,128)(2,1)} %chol_ref.3, f32[96,128]{1,0:T(8,128)} %aux_ref.1), custom_call_target="tpu_custom_call" | custom-call | flops 2952790016 | bytes 16777216 | tf_op jit(solution)/shard_map/pallas_call | solution.py:450
  58.4 96.4 %shard_map.78 = bf16[2,3072,128]{2,1,0:T(8,128)(2,1)} custom-call(bf16[96,128]{1,0:T(8,128)(2,1)} %shard_map.77.s_ref, bf16[192,96]{1,0:T(8,128)(2,1)} %constant.31.clone.perm_ref, bf16[128,256,256]{2,1,0:T(8,128)(2,1)} %chol_ref.3), custom_call_target="tpu_custom_call" | custom-call | flops 1610612736 | bytes 16777216 | tf_op jit(solution)/shard_map/pallas_call | solution.py:241
  154.8 0.0 copy-start.1
  154.8 1.2 slice.19
  156.0 0.3 reverse_select_fusion
  156.3 0.5 copy.12
  156.8 0.2 slice.16
  157.0 0.3 slice.18
  157.3 0.3 copy.18
  157.6 0.0 copy-start.2
  157.6 1.5 fusion.6
  159.1 0.5 reshape.23
  159.6 0.4 convolution_convert_fusion
  159.9 0.4 fusion
  160.3 0.4 fusion.1
  160.7 0.0 copy-start.4
  160.7 0.4 fusion.5
  161.1 0.4 copy-done.4
  161.5 0.3 convolution_bitcast_fusion
  161.8 0.9 copy.14
  (4 shorter events, 0.0 us)
Async XLA Ops:
  0.6 0.9 copy-start
  154.8 2.0 %copy-start.1 = (bf16[2,3072,128]{2,1,0:T(8,128)(2,1)S(1)}, bf16[2,3072,128]{2,1,0:T(8,128)(2,1)}, u32[]{:S(2)}) copy-start(bf16[2,3072,128]{2,1,0:T(8,128)(2,1)} %shard_map.78) | copy-start | bytes 4718596
  157.6 2.0 %copy-start.2 = (bf16[6,256,128]{2,1,0:T(8,128)(2,1)S(1)}, bf16[6,256,128]{2,1,0:T(8,128)(2,1)}, u32[]{:S(2)}) copy-start(bf16[6,256,128]{2,1,0:T(8,128)(2,1)} %param.6) | copy-start | bytes 1179652
  160.7 0.8 copy-start.4
  161.5 1.2 copy-start.3

commit v4 on v3

--- a/solution.py
+++ b/solution.py
@@ -32,7 +32,7 @@
     return order.reshape(-1)[:, None] == np.arange(2 * half)[None, :]
 
 
-def scatter_kernel(planes, chunks, s_ref, perm_ref, chol_ref, out_ref,
+def scatter_kernel(planes, chunks, ahead, s_ref, perm_ref, chol_ref, out_ref,
                    sib_s, sp, raw, turned, ysend, held, up, down,
                    s_sem, load_sem, chol_send, chol_recv, y_send, y_recv,
                    up_send, up_recv, down_send, down_recv, out_send, out_recv):
@@ -98,7 +98,7 @@
         chol_swap(k).start()
         return carry
 
-    lax.fori_loop(0, chunks, begin, 0)
+    lax.fori_loop(0, ahead, begin, 0)
     s_copy.wait()
     for parity in range(2):
         for side in range(2):
@@ -143,6 +143,10 @@
             remote(held.at[k, d], buf.at[k, d], send.at[k, d], recv.at[k, d], target).start()
 
     def step(t, carry):
+        @pl.when(t + ahead < chunks)
+        def _():
+            begin(t + ahead, 0)
+
         @pl.when(t < chunks)
         def _():
             chol_load(t).wait()
@@ -239,7 +243,7 @@
     slots = pltpu.VMEM((chunks, planes, rows, 128), bf16)
     dma = pltpu.SemaphoreType.DMA
     return pl.pallas_call(
-        functools.partial(scatter_kernel, planes, chunks),
+        functools.partial(scatter_kernel, planes, chunks, 3),
         out_shape=jax.ShapeDtypeStruct((2, norb * 12, 128), bf16),
         in_specs=[pl.BlockSpec(memory_space=pltpu.VMEM), pl.BlockSpec(memory_space=pltpu.VMEM),
                   pl.BlockSpec(memory_space=pl.ANY)],

time: 163 us -> 163 us (level)
  no operation moved by 1% of the time
where the time goes in v4:
time: 163 us
  Pallas kernels  150 us (92%)
  local copies, waits for them, and re-layouts  6.8 us (4%)
  matrix products  3.82 us (2%)
  other arithmetic  1.74 us (1%)
    pallas_call x1, Pallas kernels, reduced_potential(): pl.pallas_call(functools.partial(scatter_kernel, planes, chunks, 3), out_...  96.4 us
    pallas_call x1, Pallas kernels, shifted_fields(): pl.pallas_call(functools.partial(bias_kernel, planes), out_shape=jax.Shap...  53.2 us
    unnamed x13, local copies, waits for them, and re-layouts  4.1 us

profile of v4, /device:TPU:0, one launch (start us, length us, event | category | flops | bytes accessed | tf_op | source)
XLA Modules:
  0.0 162.8 jit_solution(7830444925381531005)
XLA Ops:
  0.6 0.0 copy-start
  0.7 0.9 copy-done
  1.6 2.1 %convolution_convert_fusion.1.rot_ref = bf16[6,128,256]{2,1,0:T(8,128)(2,1)} fusion(bf16[6,128,128]{2,1,0:T(8,128)(2,1)S(1)} %copy-done, bf16[6,256,128]{2,1,0:T(8,128)(2,1)} %param.6), kind=kOutput, calls=%fused_computation.11 | convolution fusion | flops 50528256 | bytes 983040 | tf_op jit(solution)/shard_map/wpi,wij->wjp/dot_general | solution.py:479
  3.6 1.6 copy.9
  5.2 53.2 %shard_map.77.s_ref = bf16[96,128]{1,0:T(8,128)(2,1)} custom-call(bf16[6,128,256]{2,1,0:T(8,128)(2,1)} %convolution_convert_fusion.1.rot_ref, bf16[128,256]{1,0:T(8,128)(2,1)} %bitcast.30, bf16[128,256,256]{2,1,0:T(8,128)(2,1)} %chol_ref.3, f32[96,128]{1,0:T(8,128)} %aux_ref.1), custom_call_target="tpu_custom_call" | custom-call | flops 2952790016 | bytes 16777216 | tf_op jit(solution)/shard_map/pallas_call | solution.py:454
  58.4 96.4 %shard_map.78 = bf16[2,3072,128]{2,1,0:T(8,128)(2,1)} custom-call(bf16[96,128]{1,0:T(8,128)(2,1)} %shard_map.77.s_ref, bf16[192,96]{1,0:T(8,128)(2,1)} %constant.31.clone.perm_ref, bf16[128,256,256]{2,1,0:T(8,128)(2,1)} %chol_ref.3), custom_call_target="tpu_custom_call" | custom-call | flops 1610612736 | bytes 16777216 | tf_op jit(solution)/shard_map/pallas_call | solution.py:245
  154.8 0.0 copy-start.1
  154.8 1.2 slice.19
  156.0 0.3 reverse_select_fusion
  156.3 0.5 copy.12
  156.9 0.2 slice.16
  157.1 0.3 slice.18
  157.3 0.3 copy.18
  157.6 0.0 copy-start.2
  157.6 1.5 fusion.6
  159.1 0.5 reshape.23
  159.6 0.4 convolution_convert_fusion
  160.0 0.4 fusion
  160.4 0.4 fusion.1
  160.7 0.0 copy-start.4
  160.7 0.4 fusion.5
  161.1 0.4 copy-done.4
  161.6 0.3 convolution_bitcast_fusion
  161.9 0.9 copy.14
  (4 shorter events, 0.0 us)
Async XLA Ops:
  0.6 0.9 copy-start
  154.8 2.0 %copy-start.1 = (bf16[2,3072,128]{2,1,0:T(8,128)(2,1)S(1)}, bf16[2,3072,128]{2,1,0:T(8,128)(2,1)}, u32[]{:S(2)}) copy-start(bf16[2,3072,128]{2,1,0:T(8,128)(2,1)} %shard_map.78) | copy-start | bytes 4718596
  157.6 2.0 %copy-start.2 = (bf16[6,256,128]{2,1,0:T(8,128)(2,1)S(1)}, bf16[6,256,128]{2,1,0:T(8,128)(2,1)}, u32[]{:S(2)}) copy-start(bf16[6,256,128]{2,1,0:T(8,128)(2,1)} %param.6) | copy-start | bytes 1179652
  160.7 0.8 copy-start.4
  161.6 1.2 copy-start.3

commit v5 on v4

--- a/solution.py
+++ b/solution.py
@@ -33,7 +33,7 @@
 
 
 def scatter_kernel(planes, chunks, ahead, s_ref, perm_ref, chol_ref, out_ref,
-                   sib_s, sp, raw, turned, ysend, held, up, down,
+                   sib_s, sp, raw, turned, mine, ysend, held, up, down,
                    s_sem, load_sem, chol_send, chol_recv, y_send, y_recv,
                    up_send, up_recv, down_send, down_recv, out_send, out_recv):
     own_g, norb, _ = chol_ref.shape
@@ -101,35 +101,40 @@
     lax.fori_loop(0, ahead, begin, 0)
     s_copy.wait()
     for parity in range(2):
-        for side in range(2):
-            pick = perm_ref[pl.ds((parity * 2 + side) * half, half), :]
-            sp[parity, side, :, 0:own_g] = jnp.dot(
+        for place, side in ((0, 1 - y), (1, y)):
+            pick = perm_ref[pl.ds(pl.multiple_of((parity * 2 + side) * half, 16), half), :]
+            at = pl.ds(place * half, half)
+            sp[parity, at, 0:own_g] = jnp.dot(
                 pick, s_ref[...], preferred_element_type=f32).astype(bf16)
-            sp[parity, side, :, own_g:] = jnp.dot(
+            sp[parity, at, own_g:] = jnp.dot(
                 pick, sib_s[...], preferred_element_type=f32).astype(bf16)
 
     low = lax.broadcasted_iota(jnp.int32, (8, 128), 0) < 4
 
-    def products(k, side, dst, add):
+    def products(k):
+        slot = lax.rem(k, 2)
+
         def quad(j, carry):
-            slot = lax.rem(k, 2)
-            r = [jnp.dot(sp[i % 2, side], turned[slot, j * 4 + i], preferred_element_type=f32)
+            r = [jnp.dot(sp[i % 2], turned[slot, j * 4 + i], preferred_element_type=f32)
                  for i in range(4)]
             at = pl.ds(pl.multiple_of(j * 48, 48), 48)
-            for d in range(planes):
-                pieces = []
-                mixed = slice(planes * 8 + (d // 2) * 8, planes * 8 + (d // 2) * 8 + 8)
-                for i in (0, 2):
-                    even, odd = r[i][mixed], r[i + 1][mixed]
-                    pieces += [r[i][d * 8:d * 8 + 8], r[i + 1][d * 8:d * 8 + 8],
-                               jnp.where(low, even, odd) if d % 2 == 0 else jnp.where(low, odd, even)]
-                value = jnp.concatenate(pieces, axis=0)
-                if add:
-                    value = value + dst[k, d, at].astype(f32)
-                dst[k, d, at] = value.astype(bf16)
+            for place in range(2):
+                base = place * half
+                for d in range(planes):
+                    pieces = []
+                    start, rest = base + d * 8, base + planes * 8 + (d // 2) * 8
+                    for i in (0, 2):
+                        even, odd = r[i][rest:rest + 8], r[i + 1][rest:rest + 8]
+                        pieces += [r[i][start:start + 8], r[i + 1][start:start + 8],
+                                   jnp.where(low, even, odd) if d % 2 == 0 else jnp.where(low, odd, even)]
+                    value = jnp.concatenate(pieces, axis=0).astype(bf16)
+                    if place == 0:
+                        ysend[k, d, at] = value
+                    else:
+                        mine[slot, d, at] = value
             return carry
 
-        lax.fori_loop(0, span // 4, quad, 0)
+        lax.fori_loop(0, span // 4, quad, 0, unroll=2)
 
     def hop(k, d, buf, send, recv, has_source, target):
         @pl.when(has_source)
@@ -159,14 +164,16 @@
                 return carry
 
             lax.fori_loop(0, 2 * own_g // 16, turn, 0)
-            products(t, 1 - y, ysend, False)
+            products(t)
             y_copy(t).start()
 
         @pl.when(jnp.logical_and(t >= 1, t <= chunks))
         def _():
             k = t - 1
             y_copy(k).wait_recv()
-            products(k, y, held, True)
+            slot = lax.rem(k, 2)
+            for d in range(planes):
+                held[k, d] = (held[k, d].astype(f32) + mine[slot, d].astype(f32)).astype(bf16)
 
         ku = t - 1 - z
 
@@ -250,9 +257,10 @@
         out_specs=pl.BlockSpec(memory_space=pltpu.VMEM),
         scratch_shapes=[
             pltpu.VMEM((n_walkers, own_g), bf16),
-            pltpu.VMEM((2, 2, n_walkers // 2, 2 * own_g), bf16),
+            pltpu.VMEM((2, n_walkers, 2 * own_g), bf16),
             pltpu.VMEM((2 * own_g, norb, 128), bf16),
             pltpu.VMEM((2, norb // chunks, 2 * own_g, 128), bf16),
+            pltpu.VMEM((2, planes, rows, 128), bf16),
             slots, slots, slots, slots,
             dma((2,)), dma((chunks,)), dma((chunks,)), dma((chunks,)), dma((chunks,)), dma((chunks,)),
             dma((chunks, planes)), dma((chunks, planes)), dma((chunks, planes)), dma((chunks, planes)),

time: 163 us -> 160 us (0.982)
  Pallas kernels: 150 us -> 146 us
    pallas_call x1, Pallas kernels: 96.4 us -> 93 us  [reduced_potential(): pl.pallas_call(functools.partial(scatter_kernel, planes, chunks, 3), out_...]
where the time goes in v5:
time: 160 us; the launch traced here: 159 us
  Pallas kernels  146 us (91%)
  local copies, waits for them, and re-layouts  6.8 us (4%)
  matrix products  3.82 us (2%)
  other arithmetic  1.74 us (1%)
    pallas_call x1, Pallas kernels, reduced_potential(): pl.pallas_call(functools.partial(scatter_kernel, planes, chunks, 3), out_...  93 us
    pallas_call x1, Pallas kernels, shifted_fields(): pl.pallas_call(functools.partial(bias_kernel, planes), out_shape=jax.Shap...  53.2 us
    unnamed x13, local copies, waits for them, and re-layouts  4.1 us

profile of v5, /device:TPU:0, one launch (start us, length us, event | category | flops | bytes accessed | tf_op | source)
XLA Modules:
  0.0 159.4 jit_solution(9899344922627389055)
XLA Ops:
  0.6 0.0 copy-start
  0.7 0.9 copy-done
  1.6 2.1 %convolution_convert_fusion.1.rot_ref = bf16[6,128,256]{2,1,0:T(8,128)(2,1)} fusion(bf16[6,128,128]{2,1,0:T(8,128)(2,1)S(1)} %copy-done, bf16[6,256,128]{2,1,0:T(8,128)(2,1)} %param.6), kind=kOutput, calls=%fused_computation.11 | convolution fusion | flops 50528256 | bytes 983040 | tf_op jit(solution)/shard_map/wpi,wij->wjp/dot_general | solution.py:487
  3.6 1.6 copy.9
  5.2 53.2 %shard_map.77.s_ref = bf16[96,128]{1,0:T(8,128)(2,1)} custom-call(bf16[6,128,256]{2,1,0:T(8,128)(2,1)} %convolution_convert_fusion.1.rot_ref, bf16[128,256]{1,0:T(8,128)(2,1)} %bitcast.30, bf16[128,256,256]{2,1,0:T(8,128)(2,1)} %chol_ref.3, f32[96,128]{1,0:T(8,128)} %aux_ref.1), custom_call_target="tpu_custom_call" | custom-call | flops 2952790016 | bytes 16777216 | tf_op jit(solution)/shard_map/pallas_call | solution.py:462
  58.4 93.0 %shard_map.78 = bf16[2,3072,128]{2,1,0:T(8,128)(2,1)} custom-call(bf16[96,128]{1,0:T(8,128)(2,1)} %shard_map.77.s_ref, bf16[192,96]{1,0:T(8,128)(2,1)} %constant.31.clone.perm_ref, bf16[128,256,256]{2,1,0:T(8,128)(2,1)} %chol_ref.3), custom_call_target="tpu_custom_call" | custom-call | flops 1610612736 | bytes 16777216 | tf_op jit(solution)/shard_map/pallas_call | solution.py:252
  151.4 0.0 copy-start.1
  151.4 1.2 slice.19
  152.6 0.3 reverse_select_fusion
  152.9 0.5 copy.12
  153.5 0.2 slice.16
  153.7 0.3 slice.18
  153.9 0.3 copy.18
  154.2 0.0 copy-start.2
  154.2 1.5 fusion.6
  155.7 0.5 reshape.23
  156.2 0.4 convolution_convert_fusion
  156.6 0.4 fusion
  156.9 0.4 fusion.1
  157.3 0.0 copy-start.4
  157.3 0.4 fusion.5
  157.7 0.4 copy-done.4
  158.2 0.3 convolution_bitcast_fusion
  158.5 0.9 copy.14
  (4 shorter events, 0.0 us)
Async XLA Ops:
  0.6 0.9 copy-start
  151.4 2.0 %copy-start.1 = (bf16[2,3072,128]{2,1,0:T(8,128)(2,1)S(1)}, bf16[2,3072,128]{2,1,0:T(8,128)(2,1)}, u32[]{:S(2)}) copy-start(bf16[2,3072,128]{2,1,0:T(8,128)(2,1)} %shard_map.78) | copy-start | bytes 4718596
  154.2 2.0 %copy-start.2 = (bf16[6,256,128]{2,1,0:T(8,128)(2,1)S(1)}, bf16[6,256,128]{2,1,0:T(8,128)(2,1)}, u32[]{:S(2)}) copy-start(bf16[6,256,128]{2,1,0:T(8,128)(2,1)} %param.6) | copy-start | bytes 1179652
  157.3 0.8 copy-start.4
  158.2 1.2 copy-start.3
